TPU v7x, 32 devices: a whole 2x2x4 slice. The times are simulated.
32 devices in a mesh: row: 8 (over z, x), col: 4 (over y, core).
Axes of the slice: x: 2, y: 2, z: 4, core: 2. Of those that a mesh axis runs over, the one named last changes fastest.
Arguments:
- amplitudes: bfloat16 [1024, 16384], P(('row', 'col')), may hold values from -6 to 6
- integrals: bfloat16 [16384, 1024], P('row', 'col'), may hold values from -0.125 to 0.125
- vir_irrep: int32 [1024], replicated, may hold values from 0 to 7, as said below
- occ_starts: int32 [7], replicated, may hold values from 1 to 119, as said below
- panel_owner: int32 [8, 4], replicated, may hold values from 0 to 3, each once within a row
Outputs:
- residual: float32 [1024, 1024], P(('row', 'col'))
Inputs may be any that keep to these rules, and one draw needn't show every extreme that they name: `vir_irrep`: each irrep labels exactly 128 virtual orbitals. `occ_starts`: strictly increasing; orbitals of irrep 0 start at 0. `panel_owner`: each row names each column index once.
All inputs are finite; a program needn't handle non-finite values.
Results may differ from a plain program's by a relative error of at most 0.0003.
Values may be sent and summed in bfloat16 or wider, within the bound.
A program may use at most 64 MiB of HBM per device.

v0:
```python
import jax
import jax.numpy as jnp
from jax import lax
from jax.sharding import PartitionSpec as P

NOCC = 120
A_SLAB = 1


def spread(block, axis, holder):
    block = jnp.where(lax.axis_index(axis) == holder, block, jnp.zeros_like(block))
    return lax.psum(block, axis)


def occ_labels(orbital, occ_starts):
    return jnp.sum((orbital[:, None] >= occ_starts[None, :]).astype(jnp.int32), axis=1)


def pair_irreps(first_labels, vir_irrep):
    return jnp.bitwise_xor(first_labels[:, None], vir_irrep[None, :]).reshape(-1)


def body(amplitudes, integrals, vir_irrep, occ_starts, panel_owner):
    row_total = lax.axis_size("row")
    col_total = lax.axis_size("col")
    row_place = lax.axis_index("row")
    col_place = lax.axis_index("col")
    pair_rows = amplitudes.shape[0]
    slab_rows = integrals.shape[0]
    vir_total = vir_irrep.shape[0]
    slab_orbitals = slab_rows // vir_total
    own_owner = lax.dynamic_slice_in_dim(panel_owner, row_place, 1, 0)[0]
    regrouped = lax.all_to_all(amplitudes, "row", split_axis=1, concat_axis=0, tiled=True)
    local_rows = jnp.arange(row_total * pair_rows, dtype=jnp.int32)
    source_rank = local_rows // pair_rows
    within = local_rows % pair_rows
    pair_index = (source_rank * col_total + col_place) * pair_rows + within
    pair_irrep = jnp.bitwise_xor(
        occ_labels(pair_index // NOCC, occ_starts), occ_labels(pair_index % NOCC, occ_starts)
    )
    slab_labels = lax.dynamic_slice_in_dim(vir_irrep, row_place * slab_orbitals, slab_orbitals, 0)
    slab_irrep = pair_irreps(slab_labels, vir_irrep)
    out_irrep = pair_irreps(vir_irrep[:A_SLAB], vir_irrep)
    masked_t = jnp.where(
        pair_irrep[:, None] == slab_irrep[None, :], regrouped, jnp.zeros((), regrouped.dtype)
    )
    panel_list = []
    for panel_slot in range(col_total):
        panel_list.append(spread(integrals, "col", own_owner[panel_slot]))
    ordered = jnp.concatenate(panel_list, axis=1)
    masked_v = jnp.where(
        slab_irrep[:, None] == out_irrep[None, :], ordered, jnp.zeros((), ordered.dtype)
    )
    partial_sums = jnp.dot(masked_t, masked_v, preferred_element_type=jnp.float32)
    residual = lax.psum_scatter(partial_sums, "row", scatter_dimension=0, tiled=True)
    return residual


def solution(mesh):
    in_specs = (P(("row", "col"), None), P("row", "col"), P(), P(), P())
    out_specs = P(("row", "col"), None)
    return jax.shard_map(body, mesh=mesh, in_specs=in_specs, out_specs=out_specs, check_vma=False)
```

profile of v0, /device:TPU:0, one launch (start us, length us, event | category | flops | bytes accessed | tf_op | source)
XLA Modules:
  0.0 179.5 jit_solution(8815661897112001623)
XLA Ops:
  6.5 0.0 copy-start
  6.5 0.0 all-reduce.3.cloned.1.call-start
  6.5 0.7 copy-done
  7.2 0.1 constant_dynamic-slice_fusion
  7.3 0.6 fusion.22
  10.5 3.3 %broadcast_select_fusion.3 = (bf16[2048,256]{1,0:T(8,128)(2,1)}, bf16[2048,256]{1,0:T(8,128)(2,1)}, bf16[2048,256]{1,0:T(8,128)(2,1)}, bf16[2048,256]{1,0:T(8,128)(2,1)}) fusion(bf16[2048,256]{1,0:T(8,128)(2,1)} %param.6, pred[]{:T(512)S(6)} %eq.47, pred[]{:T(512)S(6)} %eq.48, pred[]{:T(512)S(6)} %eq.50, pred[]{:T(512)S(6)} %eq.49), kind=kLoop, calls=%fused_computation.19 | loop fusion | flops 2097152 | bytes 5242884 | tf_op jit(solution)/shard_map/jit(_where)/select_n | solution.py:11
  13.8 0.0 copy-start.1
  13.8 0.0 all-reduce.3.cloned.1.call-update
  13.8 1.2 copy-done.1
  15.0 1.1 copy.13
  16.1 7.4 %all-to-all-start = ((bf16[32,8,2048]{2,0,1:T(8,128)(2,1)}), bf16[32,8,2048]{2,0,1:T(8,128)(2,1)S(1)}, u32[]{:S(2)}, u32[]{:S(2)}) async-start(bf16[32,8,2048]{2,0,1:T(8,128)(2,1)} %bitcast.15), calls=%async_computation | async-start | bytes 2097152 | tf_op jit(solution)/shard_map/all_to_all | solution.py:33
  23.5 0.0 reduce-scatter.2.cloned.1.call-start
  23.5 0.0 copy-done.2
  23.6 0.5 slice.19
  24.1 0.1 dynamic_slice.6
  24.1 0.1 xor_bitcast_fusion
  24.2 0.0 copy-done.3
  24.3 0.1 convert_reduce_fusion
  24.3 0.6 broadcast_xor_fusion
  25.0 24.3 %all-to-all-done = bf16[32,8,2048]{2,0,1:T(8,128)(2,1)S(1)} async-done(((bf16[32,8,2048]{2,0,1:T(8,128)(2,1)}), bf16[32,8,2048]{2,0,1:T(8,128)(2,1)S(1)}, u32[]{:S(2)}, u32[]{:S(2)}) %all-to-all-start) | async-done | bytes 1048608 | tf_op jit(solution)/shard_map/all_to_all | solution.py:33
  49.3 53.4 %all-reduce.3.cloned.1.call-done = (bf16[2048,256]{1,0:T(8,128)(2,1)}, bf16[2048,256]{1,0:T(8,128)(2,1)}, bf16[2048,256]{1,0:T(8,128)(2,1)}, bf16[2048,256]{1,0:T(8,128)(2,1)}) async-done(((bf16[2048,256]{1,0:T(8,128)(2,1)}, bf16[2048,256]{1,0:T(8,128)(2,1)}, bf16[2048,256]{1,0:T(8,128)(2,1)}, bf16[2048,256]{1,0:T(8,128)(2,1)}), (bf16[2048,256]{1,0:T(8,128)(2,1)}, bf16[2048,256]{1,0:T(8,128)(2,1)}, ...) | async-done | bytes 4194320 | tf_op jit(solution)/shard_map/psum | solution.py:12
  102.7 5.5 %fusion = f32[256,1024]{1,0:T(8,128)} fusion(bf16[2048,256]{1,0:T(8,128)(2,1)} %get-tuple-element.7, bf16[2048,256]{1,0:T(8,128)(2,1)} %get-tuple-element.8, bf16[2048,256]{1,0:T(8,128)(2,1)} %get-tuple-element.9, bf16[2048,256]{1,0:T(8,128)(2,1)} %get-tuple-element.10, s32[1024]{0:T(1024)S(1)} %broadcast_xor_fusion, s32[2048]{0:T(1024)S(1)} %bitcast.19, ...), kind=kOutput, calls=%fused_computation.1 | convolution fusion | flops 1095761920 | bytes 6304768 | tf_op jit(solution)/shard_map/dot_general | solution.py:54
  108.2 0.0 reduce-scatter.2.cloned.1.call-update
  108.2 64.4 %reduce-scatter.2.cloned.1.call-done = f32[32,1024]{1,0:T(8,128)} async-done(((f32[256,1024]{1,0:T(8,128)}), f32[32,1024]{1,0:T(8,128)}) %reduce-scatter.2.cloned.1.call-update) | async-done | bytes 131088 | tf_op jit(solution)/shard_map/reduce_scatter | solution.py:55
  (5 shorter events, 0.0 us)
Async XLA Ops:
  6.5 0.7 copy-start
  6.5 96.2 %all-reduce.3.cloned.1.call-start = ((), (), s32[]{:S(2)}) async-start(), calls=%async_computation.3 | async-start | bytes 8388608 | tf_op jit(solution)/shard_map/psum | solution.py:12
  13.8 1.2 copy-start.1
  16.1 7.4 %copy-start.2 = (s32[1024]{0:T(1024)S(1)}, s32[1024]{0:T(1024)}, u32[]{:S(2)}) copy-start(s32[1024]{0:T(1024)} %param.7) | copy-start | bytes 12292
  16.1 8.1 %copy-start.3 = (s32[7]{0:T(128)S(1)}, s32[7]{0:T(128)}, u32[]{:S(2)}) copy-start(s32[7]{0:T(128)} %param.8) | copy-start | bytes 88
  16.1 33.2 %all-to-all-start = ((bf16[32,8,2048]{2,0,1:T(8,128)(2,1)}), bf16[32,8,2048]{2,0,1:T(8,128)(2,1)S(1)}, u32[]{:S(2)}, u32[]{:S(2)}) async-start(bf16[32,8,2048]{2,0,1:T(8,128)(2,1)} %bitcast.15), calls=%async_computation | async-start | bytes 2097152 | tf_op jit(solution)/shard_map/all_to_all | solution.py:33
  23.5 149.1 %reduce-scatter.2.cloned.1.call-start = ((), (), s32[]{:S(2)}) async-start(), calls=%async_computation.2 | async-start | bytes 1179648 | tf_op jit(solution)/shard_map/reduce_scatter | solution.py:55
Sparse Core Ops, SparseCore 0:
  13.9 88.7 all-reduce.2
  108.4 64.2 reduce-scatter.1
where the time goes:
time: 180 us; the launch traced here: 179 us
  waiting for transfers between devices  142 us (79%)
  between operations  16 us (9%)
  starting transfers between devices  7.42 us (4%)
  matrix products  5.52 us (3%)
  local copies, waits for them, and re-layouts  4.27 us (2%)
  other arithmetic  4.12 us (2%)
    reduce_scatter x1, waiting for transfers between devices, body(): lax.psum_scatter(partial_sums, 'row', scatter_dimension=0, tiled=True)  64.4 us
    psum x1, waiting for transfers between devices, spread(): return lax.psum(block, axis)  53.4 us
    all_to_all x1, waiting for transfers between devices, body(): lax.all_to_all(amplitudes, 'row', split_axis=1, concat_axis=0, tiled=True)  24.3 us
    all_to_all x1, starting transfers between devices, body(): lax.all_to_all(amplitudes, 'row', split_axis=1, concat_axis=0, tiled=True)  7.38 us
    dot_general x1, matrix products, body(): jnp.dot(masked_t, masked_v, preferred_element_type=jnp.float32)  5.52 us
  transfers between devices with their start and end apart: 3, of which 3 were waited for; matrix products, arithmetic and copies ran while one was open for 1% of the time, Pallas kernels for 0%

commit v1 on v0

v1 whole, which is shorter than its diff:
```python
import functools

import jax
import jax.numpy as jnp
from jax import lax
from jax.experimental import pallas as pl
from jax.experimental.pallas import tpu as pltpu
from jax.sharding import PartitionSpec as P

IRREPS = 8
NOCC = 120
MESH = pl.DeviceIdType.MESH
F32 = jnp.float32
BF16 = jnp.bfloat16


def dot(a, b):
    return jnp.dot(a, b, preferred_element_type=F32)


def dot_nt(a, b):
    return lax.dot_general(a, b, (((1,), (1,)), ((), ())), preferred_element_type=F32)


def three_parts(x):
    high = x.astype(BF16)
    rest = x - high.astype(F32)
    middle = rest.astype(BF16)
    low = (rest - middle.astype(F32)).astype(BF16)
    return high, middle, low


def kernel(
    rows, cols, live,
    amp_hbm, int_hbm, vir_ref, vir_s, occ_s, owner_s,
    out_ref,
    amp, integ, tsend, tbuf, vbuf, rpart, rrecv,
    load_sem, t_send, t_recv, v_send, v_recv, r_send, r_recv,
):
    row, col = lax.axis_index("row"), lax.axis_index("col")
    pair_rows, amp_cols = amp_hbm.shape
    slab_rows, panel = int_hbm.shape
    nvir = vir_ref.shape[1]
    local_c = slab_rows // nvir
    chips = cols // 2
    chip, core = col // 2, col % 2

    load_v = pltpu.make_async_copy(int_hbm, integ, load_sem.at[0])
    load_t = pltpu.make_async_copy(amp_hbm, amp, load_sem.at[1])
    load_v.start()
    load_t.start()

    barrier = pltpu.get_barrier_semaphore()
    for o in range(1, rows):
        pl.semaphore_signal(barrier, inc=1, device_id=(lax.rem(row + o, rows), col), device_id_type=MESH)
    for o in range(1, cols):
        pl.semaphore_signal(barrier, inc=1, device_id=(row, lax.rem(col + o, cols)), device_id_type=MESH)

    vir = vir_ref[...]
    irrep_of = lax.broadcasted_iota(jnp.int32, (IRREPS, nvir), 0)
    onehot = (jnp.broadcast_to(vir, (IRREPS, nvir)) == irrep_of).astype(F32)
    tiles = nvir // 128
    onehot_tiles = [onehot[:, i * 128:(i + 1) * 128] for i in range(tiles)]
    before = (
        lax.broadcasted_iota(jnp.int32, (128, 128), 0) < lax.broadcasted_iota(jnp.int32, (128, 128), 1)
    ).astype(BF16)
    within = dot(jnp.concatenate(onehot_tiles, axis=0).astype(BF16), before)
    carry = jnp.zeros((IRREPS, 1), F32)
    rank_tiles = []
    for i in range(tiles):
        counted = within[i * IRREPS:(i + 1) * IRREPS] + carry
        rank_tiles.append(jnp.sum(onehot_tiles[i] * counted, axis=0, keepdims=True))
        carry = carry + jnp.sum(onehot_tiles[i], axis=1, keepdims=True)
    rank = jnp.concatenate(rank_tiles, axis=1).astype(jnp.int32)

    def placed(row_of_ranks):
        width = row_of_ranks.shape[1]
        return (
            jnp.broadcast_to(row_of_ranks, (live, width)) == lax.broadcasted_iota(jnp.int32, (live, width), 0)
        ).astype(F32).astype(BF16)

    place = placed(rank)

    def panel_of(values, owner):
        result = jnp.zeros((1, panel), jnp.int32)
        for slot in range(cols):
            held = (owner_s[row, slot] == owner).astype(jnp.int32)
            result = result + held * values[:, slot * panel:(slot + 1) * panel]
        return result

    def pair_irrep(first, count):
        q = first + lax.broadcasted_iota(jnp.int32, (count, 1), 0)
        i = q // NOCC
        j = q - i * NOCC
        li = jnp.zeros_like(q)
        lj = jnp.zeros_like(q)
        for n in range(IRREPS - 1):
            start = occ_s[0, n]
            li = li + (i >= start).astype(jnp.int32)
            lj = lj + (j >= start).astype(jnp.int32)
        return jnp.bitwise_xor(li, lj)

    first_label = vir_s[0, 0]

    vir_panel = panel_of(vir, col)
    vir_t = jnp.transpose(jnp.broadcast_to(vir.astype(F32), (128, nvir))).astype(jnp.int32)
    vir_t = jnp.concatenate([vir_t] * (panel // 128), axis=1)
    load_v.wait()
    for c in range(local_c):
        target = jnp.bitwise_xor(vir_panel, jnp.bitwise_xor(first_label, vir_s[0, row * local_c + c]))
        block = integ[c * nvir:(c + 1) * nvir, :]
        masked = jnp.where(vir_t == target, block.astype(F32), 0.0).astype(BF16)
        vbuf[0, c * live:(c + 1) * live, :] = dot(place, masked).astype(BF16)

    pl.semaphore_wait(barrier, rows + cols - 2)

    def send_v(source, slot, device):
        copy = pltpu.make_async_remote_copy(
            src_ref=vbuf.at[source], dst_ref=vbuf.at[slot], send_sem=v_send.at[slot], recv_sem=v_recv.at[slot],
            device_id=device, device_id_type=MESH,
        )
        copy.start()
        return copy

    sibling = (row, chip * 2 + (1 - core))
    v_copies = {}
    for o in range(1, chips):
        v_copies[2 * o] = send_v(0, 2 * o, (row, lax.rem(chip + o, chips) * 2 + core))
    v_copies[1] = send_v(0, 1, sibling)

    own_irrep = pair_irrep((row * cols + col) * pair_rows, pair_rows)
    load_t.wait()
    t_copies = []
    order = [o for o in range(1, rows)] + [0]
    group = 4
    for g in range(0, rows, group):
        offsets = order[g:g + group]
        pieces = []
        for o in offsets:
            peer = lax.rem(row + o, rows)
            for c in range(local_c):
                orbital = peer * local_c + c
                block = amp[:, pl.ds(pl.multiple_of(orbital * nvir, nvir), nvir)]
                hit = vir == jnp.bitwise_xor(own_irrep, vir_s[0, orbital])
                pieces.append(jnp.where(hit, block.astype(F32), 0.0).astype(BF16))
        packed = dot_nt(jnp.concatenate(pieces, axis=0), place).astype(BF16)
        for n, o in enumerate(offsets):
            for c in range(local_c):
                at = (n * local_c + c) * pair_rows
                kept = packed[at:at + pair_rows]
                if o == 0:
                    tbuf[0, :, c * live:(c + 1) * live] = kept
                else:
                    tsend[o - 1, :, c * live:(c + 1) * live] = kept
            if o > 0:
                copy = pltpu.make_async_remote_copy(
                    src_ref=tsend.at[o - 1], dst_ref=tbuf.at[o], send_sem=t_send.at[o], recv_sem=t_recv.at[o],
                    device_id=(lax.rem(row + o, rows), col), device_id_type=MESH,
                )
                copy.start()
                t_copies.append(copy)

    for o in range(1, chips):
        v_copies[2 * o].wait_recv()
        v_copies[2 * o + 1] = send_v(2 * o, 2 * o + 1, sibling)

    irrep_at = []
    for o in range(rows):
        source = lax.rem(row + rows - o, rows)
        irrep_at.append(pair_irrep((source * cols + col) * pair_rows, pair_rows))
    held_irrep = jnp.bitwise_xor(jnp.concatenate(irrep_at, axis=0), first_label)

    for copy in t_copies:
        copy.wait_recv()
    held = jnp.concatenate([tbuf[o] for o in range(rows)], axis=0)
    total = jnp.zeros((rows * pair_rows, live), F32)
    for slot in range(cols):
        if slot % 2 == 1:
            v_copies[slot].wait_recv()
        o, other = slot // 2, slot % 2
        holder = lax.rem(chip + chips - o, chips) * 2 + (core + other * (1 - 2 * core))
        product = dot(held, vbuf[slot])
        product = jnp.where(held_irrep == panel_of(vir, holder), product, 0.0)
        put = placed(panel_of(rank, holder))
        for part in three_parts(product):
            total = total + dot_nt(part, put)

    rpart[...] = total.reshape(rpart.shape)
    r_copies = []
    for o in range(1, rows):
        copy = pltpu.make_async_remote_copy(
            src_ref=rpart.at[o], dst_ref=rrecv.at[o], send_sem=r_send.at[o], recv_sem=r_recv.at[o],
            device_id=(lax.rem(row + rows - o, rows), col), device_id_type=MESH,
        )
        copy.start()
        r_copies.append(copy)

    result = rpart[0]
    for o in range(1, rows):
        r_copies[o - 1].wait_recv()
        result = result + rrecv[o]
    spread = jnp.zeros((pair_rows, nvir), F32)
    for part in three_parts(result):
        spread = spread + dot(part, place)
    out_ref[...] = jnp.where(jnp.bitwise_xor(own_irrep, first_label) == vir, spread, 0.0)

    for copy in list(v_copies.values()) + t_copies + r_copies:
        copy.wait_send()


def body(amplitudes, integrals, vir_irrep, occ_starts, panel_owner):
    rows, cols = lax.axis_size("row"), lax.axis_size("col")
    pair_rows, amp_cols = amplitudes.shape
    slab_rows, panel = integrals.shape
    nvir = vir_irrep.shape[0]
    live = nvir // IRREPS
    kept = (slab_rows // nvir) * live
    anywhere = pl.BlockSpec(memory_space=pl.ANY)
    vector = pl.BlockSpec(memory_space=pltpu.VMEM)
    scalars = pl.BlockSpec(memory_space=pltpu.SMEM)
    dma = pltpu.SemaphoreType.DMA
    return pl.pallas_call(
        functools.partial(kernel, rows, cols, live),
        out_shape=jax.ShapeDtypeStruct((pair_rows, cols * panel), F32),
        in_specs=[anywhere, anywhere, vector, scalars, scalars, scalars],
        out_specs=vector,
        scratch_shapes=[
            pltpu.VMEM((pair_rows, amp_cols), BF16),
            pltpu.VMEM((slab_rows, panel), BF16),
            pltpu.VMEM((rows - 1, pair_rows, kept), BF16),
            pltpu.VMEM((rows, pair_rows, kept), BF16),
            pltpu.VMEM((cols, kept, panel), BF16),
            pltpu.VMEM((rows, pair_rows, live), F32),
            pltpu.VMEM((rows, pair_rows, live), F32),
            dma((2,)),
            dma((rows,)),
            dma((rows,)),
            dma((cols,)),
            dma((cols,)),
            dma((rows,)),
            dma((rows,)),
        ],
        compiler_params=pltpu.CompilerParams(
            collective_id=0, has_side_effects=True, vmem_limit_bytes=48 * 1024 * 1024
        ),
    )(
        amplitudes, integrals, vir_irrep.reshape(1, nvir), vir_irrep.reshape(1, nvir),
        occ_starts.reshape(1, -1), panel_owner,
    )


def solution(mesh):
    in_specs = (P(("row", "col"), None), P("row", "col"), P(), P(), P())
    out_specs = P(("row", "col"), None)
    return jax.shard_map(body, mesh=mesh, in_specs=in_specs, out_specs=out_specs, check_vma=False)
```

time: 180 us -> 24.1 us (0.13)
  waiting for transfers between devices: 142 us -> 0 us
  Pallas kernels: 0 us -> 19.4 us
  between operations: 16 us -> 0.01 us
  starting transfers between devices: 7.42 us -> 0 us
  matrix products: 5.52 us -> 0 us
  other arithmetic: 4.12 us -> 0 us
    reduce_scatter x1 -> x0, waiting for transfers between devices: 64.4 us -> none  [body(): lax.psum_scatter(partial_sums, 'row', scatter_dimension=0, tiled=True)]
    psum x1 -> x0, waiting for transfers between devices: 53.4 us -> none  [spread(): return lax.psum(block, axis)]
    all_to_all x1 -> x0, waiting for transfers between devices: 24.3 us -> none  [body(): lax.all_to_all(amplitudes, 'row', split_axis=1, concat_axis=0, tiled=True)]
    pallas_call x0 -> x1, Pallas kernels: none -> 19.4 us  [body(): pl.pallas_call(functools.partial(kernel, rows, cols, live), out_shape=jax...]
    all_to_all x1 -> x0, starting transfers between devices: 7.38 us -> none  [body(): lax.all_to_all(amplitudes, 'row', split_axis=1, concat_axis=0, tiled=True)]
    dot_general x1 -> x0, matrix products: 5.52 us -> none  [body(): jnp.dot(masked_t, masked_v, preferred_element_type=jnp.float32)]
    select_n x2 -> x0, other arithmetic: 3.31 us -> none  [the longest x1 3.29 us: spread(): jnp.where(lax.axis_index(axis) == holder, block, jnp.zeros_like(block))]
    unnamed x9 -> x12, local copies, waits for them, and re-layouts: 1.89 us -> 4.44 us
  transfers between devices with their start and end apart: 3 -> 0, of which waited for: 3 -> 0; matrix products, arithmetic and copies ran while one was open for 1% -> 0% of each run, Pallas kernels for 0% -> 0%
where the time goes in v1:
time: 24.1 us; the launch traced here: 23.9 us
  Pallas kernels  19.4 us (80%)
  local copies, waits for them, and re-layouts  4.44 us (18%)
    pallas_call x1, Pallas kernels, body(): pl.pallas_call(functools.partial(kernel, rows, cols, live), out_shape=jax...  19.4 us
    unnamed x12, local copies, waits for them, and re-layouts  4.44 us

profile of v1, /device:TPU:0, one launch (start us, length us, event | category | flops | bytes accessed | tf_op | source)
XLA Modules:
  0.0 23.9 jit_solution(12795804407723341930)
XLA Ops:
  0.0 0.0 copy-start.4
  0.0 0.0 copy-start.2
  0.0 0.7 %copy-done.4 = s32[8,4]{0,1:T(4,128)S(1)} copy-done((s32[8,4]{0,1:T(4,128)S(1)}, s32[8,4]{0,1:T(4,128)}, u32[]{:S(2)}) %copy-start.4) | copy-done | bytes 152
  0.7 0.0 copy-start.3
  0.7 0.1 copy.6.owner_s
  0.8 0.0 copy-done.2
  0.8 0.6 %copy-done.3 = s32[7]{0:T(128)S(1)} copy-done((s32[7]{0:T(128)S(1)}, s32[7]{0:T(128)}, u32[]{:S(2)}) %copy-start.3) | copy-done | bytes 52
  1.3 0.0 copy-start
  1.3 1.2 %copy-done = bf16[32,16384]{1,0:T(8,128)(2,1)S(1)} copy-done((bf16[32,16384]{1,0:T(8,128)(2,1)S(1)}, bf16[32,16384]{1,0:T(8,128)(2,1)}, u32[]{:S(2)}) %copy-start) | copy-done | bytes 1048600
  2.6 0.0 copy-start.1
  2.6 1.2 %copy-done.1 = bf16[2048,256]{1,0:T(8,128)(2,1)S(1)} copy-done((bf16[2048,256]{1,0:T(8,128)(2,1)S(1)}, bf16[2048,256]{1,0:T(8,128)(2,1)}, u32[]{:S(2)}) %copy-start.1) | copy-done | bytes 1048600
  3.8 19.4 %shard_map.55 = f32[32,1024]{1,0:T(8,128)S(1)} custom-call(bf16[32,16384]{1,0:T(8,128)(2,1)S(1)} %copy-done, bf16[2048,256]{1,0:T(8,128)(2,1)S(1)} %copy-done.1, s32[1,1024]{1,0:T(1,128)S(1)} %bitcast.2, s32[1,1024]{1,0:T(1,128)S(1)} %bitcast.3, s32[1,7]{1,0:T(1,128)S(1)} %bitcast.4, s32[8,4]{1,0:T(8,128)S(1)} %copy.6.owner_s), custom_call_target="tpu_custom_call" | custom-call | tf_op jit(solution)/shard_map/pallas_call | solution.py:222
  23.2 0.7 %copy.8 = f32[32,1024]{1,0:T(8,128)} copy(f32[32,1024]{1,0:T(8,128)S(1)} %shard_map.55) | data formatting | bytes 262144
Async XLA Ops:
  0.0 0.7 %copy-start.4 = (s32[8,4]{0,1:T(4,128)S(1)}, s32[8,4]{0,1:T(4,128)}, u32[]{:S(2)}) copy-start(s32[8,4]{0,1:T(4,128)} %param.9) | copy-start | bytes 388
  0.0 0.8 %copy-start.2 = (s32[1024]{0:T(1024)S(1)}, s32[1024]{0:T(1024)}, u32[]{:S(2)}) copy-start(s32[1024]{0:T(1024)} %param.7) | copy-start | bytes 12292
  0.7 0.7 %copy-start.3 = (s32[7]{0:T(128)S(1)}, s32[7]{0:T(128)}, u32[]{:S(2)}) copy-start(s32[7]{0:T(128)} %param.8) | copy-start | bytes 88
  1.3 1.2 %copy-start = (bf16[32,16384]{1,0:T(8,128)(2,1)S(1)}, bf16[32,16384]{1,0:T(8,128)(2,1)}, u32[]{:S(2)}) copy-start(bf16[32,16384]{1,0:T(8,128)(2,1)} %amp_hbm.1) | copy-start | bytes 3145732
  2.6 1.2 %copy-start.1 = (bf16[2048,256]{1,0:T(8,128)(2,1)S(1)}, bf16[2048,256]{1,0:T(8,128)(2,1)}, u32[]{:S(2)}) copy-start(bf16[2048,256]{1,0:T(8,128)(2,1)} %int_hbm.1) | copy-start | bytes 3145732

commit v2 on v1

--- a/solution.py
+++ b/solution.py
@@ -30,31 +30,49 @@
     return high, middle, low
 
 
+def remote(source, target, send_sem, recv_sem, device):
+    copy = pltpu.make_async_remote_copy(
+        src_ref=source, dst_ref=target, send_sem=send_sem, recv_sem=recv_sem,
+        device_id=device, device_id_type=MESH,
+    )
+    copy.start()
+    return copy
+
+
 def kernel(
     rows, cols, live,
-    amp_hbm, int_hbm, vir_ref, vir_s, occ_s, owner_s,
+    amp_hbm, int_hbm, vir_hbm, occ_hbm, owner_hbm,
     out_ref,
-    amp, integ, tsend, tbuf, vbuf, rpart, rrecv,
+    vir_ref, vir_s, occ_s, owner_s, amp, integ, tsend, tbuf, vbuf, rpart, rrecv,
     load_sem, t_send, t_recv, v_send, v_recv, r_send, r_recv,
 ):
     row, col = lax.axis_index("row"), lax.axis_index("col")
     pair_rows, amp_cols = amp_hbm.shape
     slab_rows, panel = int_hbm.shape
-    nvir = vir_ref.shape[1]
+    nvir = vir_hbm.shape[1]
     local_c = slab_rows // nvir
     chips = cols // 2
     chip, core = col // 2, col % 2
 
-    load_v = pltpu.make_async_copy(int_hbm, integ, load_sem.at[0])
-    load_t = pltpu.make_async_copy(amp_hbm, amp, load_sem.at[1])
-    load_v.start()
-    load_t.start()
+    loads = [
+        pltpu.make_async_copy(source, target, load_sem.at[n])
+        for n, (source, target) in enumerate((
+            (vir_hbm, vir_ref), (vir_hbm, vir_s), (occ_hbm, occ_s), (owner_hbm, owner_s),
+            (int_hbm, integ), (amp_hbm, amp),
+        ))
+    ]
+    for load in loads:
+        load.start()
+    load_v, load_t = loads[-2:]
 
     barrier = pltpu.get_barrier_semaphore()
     for o in range(1, rows):
         pl.semaphore_signal(barrier, inc=1, device_id=(lax.rem(row + o, rows), col), device_id_type=MESH)
     for o in range(1, cols):
         pl.semaphore_signal(barrier, inc=1, device_id=(row, lax.rem(col + o, cols)), device_id_type=MESH)
+
+    for load in loads[:-2]:
+        load.wait()
 
     vir = vir_ref[...]
     irrep_of = lax.broadcasted_iota(jnp.int32, (IRREPS, nvir), 0)
@@ -84,7 +102,7 @@
     def panel_of(values, owner):
         result = jnp.zeros((1, panel), jnp.int32)
         for slot in range(cols):
-            held = (owner_s[row, slot] == owner).astype(jnp.int32)
+            held = (owner_s[slot, row] == owner).astype(jnp.int32)
             result = result + held * values[:, slot * panel:(slot + 1) * panel]
         return result
 
@@ -115,12 +133,7 @@
     pl.semaphore_wait(barrier, rows + cols - 2)
 
     def send_v(source, slot, device):
-        copy = pltpu.make_async_remote_copy(
-            src_ref=vbuf.at[source], dst_ref=vbuf.at[slot], send_sem=v_send.at[slot], recv_sem=v_recv.at[slot],
-            device_id=device, device_id_type=MESH,
-        )
-        copy.start()
-        return copy
+        return remote(vbuf.at[source], vbuf.at[slot], v_send.at[slot], v_recv.at[slot], device)
 
     sibling = (row, chip * 2 + (1 - core))
     v_copies = {}
@@ -153,12 +166,9 @@
                 else:
                     tsend[o - 1, :, c * live:(c + 1) * live] = kept
             if o > 0:
-                copy = pltpu.make_async_remote_copy(
-                    src_ref=tsend.at[o - 1], dst_ref=tbuf.at[o], send_sem=t_send.at[o], recv_sem=t_recv.at[o],
-                    device_id=(lax.rem(row + o, rows), col), device_id_type=MESH,
-                )
-                copy.start()
-                t_copies.append(copy)
+                t_copies.append(remote(
+                    tsend.at[o - 1], tbuf.at[o], t_send.at[o], t_recv.at[o], (lax.rem(row + o, rows), col)
+                ))
 
     for o in range(1, chips):
         v_copies[2 * o].wait_recv()
@@ -188,12 +198,9 @@
     rpart[...] = total.reshape(rpart.shape)
     r_copies = []
     for o in range(1, rows):
-        copy = pltpu.make_async_remote_copy(
-            src_ref=rpart.at[o], dst_ref=rrecv.at[o], send_sem=r_send.at[o], recv_sem=r_recv.at[o],
-            device_id=(lax.rem(row + rows - o, rows), col), device_id_type=MESH,
-        )
-        copy.start()
-        r_copies.append(copy)
+        r_copies.append(remote(
+            rpart.at[o], rrecv.at[o], r_send.at[o], r_recv.at[o], (lax.rem(row + rows - o, rows), col)
+        ))
 
     result = rpart[0]
     for o in range(1, rows):
@@ -217,14 +224,17 @@
     kept = (slab_rows // nvir) * live
     anywhere = pl.BlockSpec(memory_space=pl.ANY)
     vector = pl.BlockSpec(memory_space=pltpu.VMEM)
-    scalars = pl.BlockSpec(memory_space=pltpu.SMEM)
     dma = pltpu.SemaphoreType.DMA
     return pl.pallas_call(
         functools.partial(kernel, rows, cols, live),
         out_shape=jax.ShapeDtypeStruct((pair_rows, cols * panel), F32),
-        in_specs=[anywhere, anywhere, vector, scalars, scalars, scalars],
+        in_specs=[anywhere] * 5,
         out_specs=vector,
         scratch_shapes=[
+            pltpu.VMEM((1, nvir), jnp.int32),
+            pltpu.SMEM((1, nvir), jnp.int32),
+            pltpu.SMEM((1, IRREPS - 1), jnp.int32),
+            pltpu.SMEM((cols, rows), jnp.int32),
             pltpu.VMEM((pair_rows, amp_cols), BF16),
             pltpu.VMEM((slab_rows, panel), BF16),
             pltpu.VMEM((rows - 1, pair_rows, kept), BF16),
@@ -232,7 +242,7 @@
             pltpu.VMEM((cols, kept, panel), BF16),
             pltpu.VMEM((rows, pair_rows, live), F32),
             pltpu.VMEM((rows, pair_rows, live), F32),
-            dma((2,)),
+            dma((6,)),
             dma((rows,)),
             dma((rows,)),
             dma((cols,)),
@@ -241,11 +251,10 @@
             dma((rows,)),
         ],
         compiler_params=pltpu.CompilerParams(
-            collective_id=0, has_side_effects=True, vmem_limit_bytes=48 * 1024 * 1024
+            collective_id=0, has_side_effects=True, vmem_limit_bytes=62 * 1024 * 1024
         ),
     )(
-        amplitudes, integrals, vir_irrep.reshape(1, nvir), vir_irrep.reshape(1, nvir),
-        occ_starts.reshape(1, -1), panel_owner,
+        amplitudes, integrals, vir_irrep.reshape(1, nvir), occ_starts.reshape(1, -1), panel_owner.T,
     )
 
 

time: 24.1 us -> 21 us (0.87)
  local copies, waits for them, and re-layouts: 4.44 us -> 1.57 us
    unnamed x12 -> x1, local copies, waits for them, and re-layouts: 4.44 us -> 1.57 us
where the time goes in v2:
time: 21 us; the launch traced here: 20.8 us
  Pallas kernels  19.2 us (91%)
  local copies, waits for them, and re-layouts  1.57 us (7%)
    pallas_call x1, Pallas kernels, body(): pl.pallas_call(functools.partial(kernel, rows, cols, live), out_shape=jax...  19.2 us
    unnamed x1, local copies, waits for them, and re-layouts  1.57 us

profile of v2, /device:TPU:0, one launch (start us, length us, event | category | flops | bytes accessed | tf_op | source)
XLA Modules:
  0.0 20.8 jit_solution(5478828113622255888)
XLA Ops:
  0.0 19.2 %shard_map.55 = f32[32,1024]{1,0:T(8,128)} custom-call(bf16[32,16384]{1,0:T(8,128)(2,1)} %amp_hbm.1, bf16[2048,256]{1,0:T(8,128)(2,1)} %int_hbm.1, s32[1,1024]{1,0:T(1,128)} %bitcast.3, s32[1,7]{1,0:T(1,128)} %bitcast.5, s32[4,8]{1,0:T(4,128)} %bitcast.4), custom_call_target="tpu_custom_call" | custom-call | tf_op jit(solution)/shard_map/pallas_call | solution.py:228
  19.2 1.6 %copy.7 = f32[32,1024]{1,0:T(8,128)} copy(f32[32,1024]{1,0:T(8,128)} %shard_map.55) | data formatting | bytes 262144

commit v3 on v2

--- a/solution.py
+++ b/solution.py
@@ -54,16 +54,21 @@
     chips = cols // 2
     chip, core = col // 2, col % 2
 
-    loads = [
-        pltpu.make_async_copy(source, target, load_sem.at[n])
-        for n, (source, target) in enumerate((
-            (vir_hbm, vir_ref), (vir_hbm, vir_s), (occ_hbm, occ_s), (owner_hbm, owner_s),
-            (int_hbm, integ), (amp_hbm, amp),
-        ))
-    ]
+    order = [o for o in range(1, rows)] + [0]
+    wide = local_c * nvir
+    pairs = [(vir_hbm, vir_ref), (vir_hbm, vir_s), (occ_hbm, occ_s), (owner_hbm, owner_s)]
+    small = len(pairs)
+    for c in range(local_c):
+        strip = pl.ds(c * nvir, nvir)
+        pairs.append((int_hbm.at[strip], integ.at[strip]))
+    for o in order:
+        strip = pl.ds(pl.multiple_of(lax.rem(row + o, rows) * wide, wide), wide)
+        pairs.append((amp_hbm.at[:, strip], amp.at[o]))
+    loads = [pltpu.make_async_copy(source, target, load_sem.at[n]) for n, (source, target) in enumerate(pairs)]
     for load in loads:
         load.start()
-    load_v, load_t = loads[-2:]
+    load_v = loads[small:small + local_c]
+    load_t = dict(zip(order, loads[small + local_c:]))
 
     barrier = pltpu.get_barrier_semaphore()
     for o in range(1, rows):
@@ -71,7 +76,7 @@
     for o in range(1, cols):
         pl.semaphore_signal(barrier, inc=1, device_id=(row, lax.rem(col + o, cols)), device_id_type=MESH)
 
-    for load in loads[:-2]:
+    for load in loads[:small]:
         load.wait()
 
     vir = vir_ref[...]
@@ -123,8 +128,8 @@
     vir_panel = panel_of(vir, col)
     vir_t = jnp.transpose(jnp.broadcast_to(vir.astype(F32), (128, nvir))).astype(jnp.int32)
     vir_t = jnp.concatenate([vir_t] * (panel // 128), axis=1)
-    load_v.wait()
-    for c in range(local_c):
+    for c in range(local_c):
+        load_v[c].wait()
         target = jnp.bitwise_xor(vir_panel, jnp.bitwise_xor(first_label, vir_s[0, row * local_c + c]))
         block = integ[c * nvir:(c + 1) * nvir, :]
         masked = jnp.where(vir_t == target, block.astype(F32), 0.0).astype(BF16)
@@ -132,28 +137,31 @@
 
     pl.semaphore_wait(barrier, rows + cols - 2)
 
-    def send_v(source, slot, device):
-        return remote(vbuf.at[source], vbuf.at[slot], v_send.at[slot], v_recv.at[slot], device)
+    def send_v(source, slot, c, device):
+        strip = pl.ds(c * live, live)
+        return remote(
+            vbuf.at[source, strip], vbuf.at[slot, strip], v_send.at[slot, c], v_recv.at[slot, c], device
+        )
 
     sibling = (row, chip * 2 + (1 - core))
     v_copies = {}
-    for o in range(1, chips):
-        v_copies[2 * o] = send_v(0, 2 * o, (row, lax.rem(chip + o, chips) * 2 + core))
-    v_copies[1] = send_v(0, 1, sibling)
+    for c in range(local_c):
+        for o in range(1, chips):
+            v_copies[2 * o, c] = send_v(0, 2 * o, c, (row, lax.rem(chip + o, chips) * 2 + core))
+        v_copies[1, c] = send_v(0, 1, c, sibling)
 
     own_irrep = pair_irrep((row * cols + col) * pair_rows, pair_rows)
-    load_t.wait()
-    t_copies = []
-    order = [o for o in range(1, rows)] + [0]
-    group = 4
+    t_copies = {}
+    group = 2
     for g in range(0, rows, group):
         offsets = order[g:g + group]
         pieces = []
         for o in offsets:
             peer = lax.rem(row + o, rows)
+            load_t[o].wait()
             for c in range(local_c):
                 orbital = peer * local_c + c
-                block = amp[:, pl.ds(pl.multiple_of(orbital * nvir, nvir), nvir)]
+                block = amp[o, :, c * nvir:(c + 1) * nvir]
                 hit = vir == jnp.bitwise_xor(own_irrep, vir_s[0, orbital])
                 pieces.append(jnp.where(hit, block.astype(F32), 0.0).astype(BF16))
         packed = dot_nt(jnp.concatenate(pieces, axis=0), place).astype(BF16)
@@ -166,13 +174,14 @@
                 else:
                     tsend[o - 1, :, c * live:(c + 1) * live] = kept
             if o > 0:
-                t_copies.append(remote(
+                t_copies[o] = remote(
                     tsend.at[o - 1], tbuf.at[o], t_send.at[o], t_recv.at[o], (lax.rem(row + o, rows), col)
-                ))
-
-    for o in range(1, chips):
-        v_copies[2 * o].wait_recv()
-        v_copies[2 * o + 1] = send_v(2 * o, 2 * o + 1, sibling)
+                )
+
+    for c in range(local_c):
+        for o in range(1, chips):
+            v_copies[2 * o, c].wait_recv()
+            v_copies[2 * o + 1, c] = send_v(2 * o, 2 * o + 1, c, sibling)
 
     irrep_at = []
     for o in range(rows):
@@ -180,27 +189,36 @@
         irrep_at.append(pair_irrep((source * cols + col) * pair_rows, pair_rows))
     held_irrep = jnp.bitwise_xor(jnp.concatenate(irrep_at, axis=0), first_label)
 
-    for copy in t_copies:
-        copy.wait_recv()
-    held = jnp.concatenate([tbuf[o] for o in range(rows)], axis=0)
-    total = jnp.zeros((rows * pair_rows, live), F32)
+    panel_irrep, panel_place = [], []
     for slot in range(cols):
-        if slot % 2 == 1:
-            v_copies[slot].wait_recv()
         o, other = slot // 2, slot % 2
         holder = lax.rem(chip + chips - o, chips) * 2 + (core + other * (1 - 2 * core))
-        product = dot(held, vbuf[slot])
-        product = jnp.where(held_irrep == panel_of(vir, holder), product, 0.0)
-        put = placed(panel_of(rank, holder))
-        for part in three_parts(product):
-            total = total + dot_nt(part, put)
-
-    rpart[...] = total.reshape(rpart.shape)
+        panel_irrep.append(panel_of(vir, holder))
+        panel_place.append(placed(panel_of(rank, holder)))
     r_copies = []
-    for o in range(1, rows):
-        r_copies.append(remote(
-            rpart.at[o], rrecv.at[o], r_send.at[o], r_recv.at[o], (lax.rem(row + rows - o, rows), col)
-        ))
+    half = rows // 2
+    for first in range(0, rows, half):
+        offsets = range(first, first + half)
+        for o in offsets:
+            if o > 0:
+                t_copies[o].wait_recv()
+        span = slice(first * pair_rows, (first + half) * pair_rows)
+        held = jnp.concatenate([tbuf[o] for o in offsets], axis=0)
+        total = jnp.zeros((half * pair_rows, live), F32)
+        for slot in range(cols):
+            if slot % 2 == 1 and first == 0:
+                for c in range(local_c):
+                    v_copies[slot, c].wait_recv()
+            product = dot(held, vbuf[slot])
+            product = jnp.where(held_irrep[span] == panel_irrep[slot], product, 0.0)
+            for part in three_parts(product):
+                total = total + dot_nt(part, panel_place[slot])
+        for n, o in enumerate(offsets):
+            rpart[o] = total[n * pair_rows:(n + 1) * pair_rows]
+            if o > 0:
+                r_copies.append(remote(
+                    rpart.at[o], rrecv.at[o], r_send.at[o], r_recv.at[o], (lax.rem(row + rows - o, rows), col)
+                ))
 
     result = rpart[0]
     for o in range(1, rows):
@@ -211,7 +229,7 @@
         spread = spread + dot(part, place)
     out_ref[...] = jnp.where(jnp.bitwise_xor(own_irrep, first_label) == vir, spread, 0.0)
 
-    for copy in list(v_copies.values()) + t_copies + r_copies:
+    for copy in list(v_copies.values()) + list(t_copies.values()) + r_copies:
         copy.wait_send()
 
 
@@ -235,18 +253,18 @@
             pltpu.SMEM((1, nvir), jnp.int32),
             pltpu.SMEM((1, IRREPS - 1), jnp.int32),
             pltpu.SMEM((cols, rows), jnp.int32),
-            pltpu.VMEM((pair_rows, amp_cols), BF16),
+            pltpu.VMEM((rows, pair_rows, amp_cols // rows), BF16),
             pltpu.VMEM((slab_rows, panel), BF16),
             pltpu.VMEM((rows - 1, pair_rows, kept), BF16),
             pltpu.VMEM((rows, pair_rows, kept), BF16),
             pltpu.VMEM((cols, kept, panel), BF16),
             pltpu.VMEM((rows, pair_rows, live), F32),
             pltpu.VMEM((rows, pair_rows, live), F32),
-            dma((6,)),
-            dma((rows,)),
-            dma((rows,)),
-            dma((cols,)),
-            dma((cols,)),
+            dma((4 + slab_rows // nvir + rows,)),
+            dma((rows,)),
+            dma((rows,)),
+            dma((cols, slab_rows // nvir)),
+            dma((cols, slab_rows // nvir)),
             dma((rows,)),
             dma((rows,)),
         ],

time: 21 us -> 20.8 us (level)
  no operation moved by 1% of the time
where the time goes in v3:
time: 20.8 us; the launch traced here: 20.7 us
  Pallas kernels  19.1 us (92%)
  local copies, waits for them, and re-layouts  1.57 us (8%)
    pallas_call x1, Pallas kernels, body(): pl.pallas_call(functools.partial(kernel, rows, cols, live), out_shape=jax...  19.1 us
    unnamed x1, local copies, waits for them, and re-layouts  1.57 us

profile of v3, /device:TPU:0, one launch (start us, length us, event | category | flops | bytes accessed | tf_op | source)
XLA Modules:
  0.0 20.7 jit_solution(2183775193264030126)
XLA Ops:
  0.0 19.1 %shard_map.55 = f32[32,1024]{1,0:T(8,128)} custom-call(bf16[32,16384]{1,0:T(8,128)(2,1)} %amp_hbm.1, bf16[2048,256]{1,0:T(8,128)(2,1)} %int_hbm.1, s32[1,1024]{1,0:T(1,128)} %bitcast.3, s32[1,7]{1,0:T(1,128)} %bitcast.5, s32[4,8]{1,0:T(4,128)} %bitcast.4), custom_call_target="tpu_custom_call" | custom-call | tf_op jit(solution)/shard_map/pallas_call | solution.py:246
  19.1 1.6 %copy.7 = f32[32,1024]{1,0:T(8,128)} copy(f32[32,1024]{1,0:T(8,128)} %shard_map.55) | data formatting | bytes 262144

commit v4 on v3

--- a/solution.py
+++ b/solution.py
@@ -125,6 +125,14 @@
 
     first_label = vir_s[0, 0]
 
+    def send_v(source, slot, c, device):
+        strip = pl.ds(c * live, live)
+        return remote(
+            vbuf.at[source, strip], vbuf.at[slot, strip], v_send.at[slot, c], v_recv.at[slot, c], device
+        )
+
+    sibling = (row, chip * 2 + (1 - core))
+    v_copies = {}
     vir_panel = panel_of(vir, col)
     vir_t = jnp.transpose(jnp.broadcast_to(vir.astype(F32), (128, nvir))).astype(jnp.int32)
     vir_t = jnp.concatenate([vir_t] * (panel // 128), axis=1)
@@ -134,18 +142,8 @@
         block = integ[c * nvir:(c + 1) * nvir, :]
         masked = jnp.where(vir_t == target, block.astype(F32), 0.0).astype(BF16)
         vbuf[0, c * live:(c + 1) * live, :] = dot(place, masked).astype(BF16)
-
-    pl.semaphore_wait(barrier, rows + cols - 2)
-
-    def send_v(source, slot, c, device):
-        strip = pl.ds(c * live, live)
-        return remote(
-            vbuf.at[source, strip], vbuf.at[slot, strip], v_send.at[slot, c], v_recv.at[slot, c], device
-        )
-
-    sibling = (row, chip * 2 + (1 - core))
-    v_copies = {}
-    for c in range(local_c):
+        if c == 0:
+            pl.semaphore_wait(barrier, rows + cols - 2)
         for o in range(1, chips):
             v_copies[2 * o, c] = send_v(0, 2 * o, c, (row, lax.rem(chip + o, chips) * 2 + core))
         v_copies[1, c] = send_v(0, 1, c, sibling)

time: 20.8 us -> 20.7 us (level)
  no operation moved by 1% of the time
where the time goes in v4:
time: 20.7 us; the launch traced here: 20.5 us
  Pallas kernels  18.9 us (91%)
  local copies, waits for them, and re-layouts  1.57 us (8%)
    pallas_call x1, Pallas kernels, body(): pl.pallas_call(functools.partial(kernel, rows, cols, live), out_shape=jax...  18.9 us
    unnamed x1, local copies, waits for them, and re-layouts  1.57 us

profile of v4, /device:TPU:0, one launch (start us, length us, event | category | flops | bytes accessed | tf_op | source)
XLA Modules:
  0.0 20.5 jit_solution(5734228588946997355)
XLA Ops:
  0.0 18.9 %shard_map.55 = f32[32,1024]{1,0:T(8,128)} custom-call(bf16[32,16384]{1,0:T(8,128)(2,1)} %amp_hbm.1, bf16[2048,256]{1,0:T(8,128)(2,1)} %int_hbm.1, s32[1,1024]{1,0:T(1,128)} %bitcast.3, s32[1,7]{1,0:T(1,128)} %bitcast.5, s32[4,8]{1,0:T(4,128)} %bitcast.4), custom_call_target="tpu_custom_call" | custom-call | tf_op jit(solution)/shard_map/pallas_call | solution.py:244
  18.9 1.6 %copy.7 = f32[32,1024]{1,0:T(8,128)} copy(f32[32,1024]{1,0:T(8,128)} %shard_map.55) | data formatting | bytes 262144

commit v5 on v4

--- a/solution.py
+++ b/solution.py
@@ -176,11 +176,6 @@
                     tsend.at[o - 1], tbuf.at[o], t_send.at[o], t_recv.at[o], (lax.rem(row + o, rows), col)
                 )
 
-    for c in range(local_c):
-        for o in range(1, chips):
-            v_copies[2 * o, c].wait_recv()
-            v_copies[2 * o + 1, c] = send_v(2 * o, 2 * o + 1, c, sibling)
-
     irrep_at = []
     for o in range(rows):
         source = lax.rem(row + rows - o, rows)
@@ -193,6 +188,12 @@
         holder = lax.rem(chip + chips - o, chips) * 2 + (core + other * (1 - 2 * core))
         panel_irrep.append(panel_of(vir, holder))
         panel_place.append(placed(panel_of(rank, holder)))
+
+    for c in range(local_c):
+        for o in range(1, chips):
+            v_copies[2 * o, c].wait_recv()
+            v_copies[2 * o + 1, c] = send_v(2 * o, 2 * o + 1, c, sibling)
+
     r_copies = []
     half = rows // 2
     for first in range(0, rows, half):

time: 20.7 us -> 20.7 us (level)
  no operation moved by 1% of the time
where the time goes in v5:
time: 20.7 us; the launch traced here: 20.5 us
  Pallas kernels  18.9 us (91%)
  local copies, waits for them, and re-layouts  1.57 us (8%)
    pallas_call x1, Pallas kernels, body(): pl.pallas_call(functools.partial(kernel, rows, cols, live), out_shape=jax...  18.9 us
    unnamed x1, local copies, waits for them, and re-layouts  1.57 us

profile of v5, /device:TPU:0, one launch (start us, length us, event | category | flops | bytes accessed | tf_op | source)
XLA Modules:
  0.0 20.5 jit_solution(286029476655367654)
XLA Ops:
  0.0 18.9 %shard_map.55 = f32[32,1024]{1,0:T(8,128)} custom-call(bf16[32,16384]{1,0:T(8,128)(2,1)} %amp_hbm.1, bf16[2048,256]{1,0:T(8,128)(2,1)} %int_hbm.1, s32[1,1024]{1,0:T(1,128)} %bitcast.3, s32[1,7]{1,0:T(1,128)} %bitcast.5, s32[4,8]{1,0:T(4,128)} %bitcast.4), custom_call_target="tpu_custom_call" | custom-call | tf_op jit(solution)/shard_map/pallas_call | solution.py:245
  18.9 1.6 %copy.7 = f32[32,1024]{1,0:T(8,128)} copy(f32[32,1024]{1,0:T(8,128)} %shard_map.55) | data formatting | bytes 262144
